TPU v7x, 32 devices: a whole 2x2x4 slice. The times are simulated.
32 devices in a mesh: grp: 2 (over x), tile: 16 (over z, y, core).
Axes of the slice: x: 2, y: 2, z: 4, core: 2. Of those that a mesh axis runs over, the one named last changes fastest.
Arguments:
- acts: bfloat16 [256, 4096], P(('grp', 'tile')), parts along dimension 0, may hold values from -6 to 6
- grads: bfloat16 [256, 4096], P(('grp', 'tile')), parts along dimension 0, may hold values from -6 to 6
- basis_in: bfloat16 [4096, 4096], P('tile'), may hold values from -0.09375 to 0.09375
- basis_out: bfloat16 [4096, 4096], P('tile'), may hold values from -0.09375 to 0.09375
Outputs:
- corr_tiles: float32 [32, 512, 2048], P(('grp', 'tile')), parts along dimension 0
There are 2 independent parts, one for each index of `grp`. A program takes and returns all parts, laid end to end along the dimension named above; an argument that names none is the same for every part. Nothing has to cross between parts.
All inputs are finite; a program needn't handle non-finite values.
Results may differ from a plain program's by a relative error of at most 0.005.
Values may be sent and summed in bfloat16 or wider, within the bound.
A program may use at most 128 MiB of HBM per device.

v0:
```python
import jax
import jax.numpy as jnp
from jax import lax
from jax.sharding import PartitionSpec as P

SEQ = 128
ROWB = 8


def body(acts, grads, basis_in, basis_out):
    tiles = lax.axis_size("tile")
    tok_rows = acts.shape[0]
    width_in = acts.shape[1]
    width_out = grads.shape[1]
    col_blocks = tiles // ROWB
    tile_rows_n = width_out // ROWB
    tile_cols_n = width_in // col_blocks
    acts_feat, grads_feat = (
        lax.all_to_all(acts, "tile", split_axis=1, concat_axis=0, tiled=True),
        lax.all_to_all(grads, "tile", split_axis=1, concat_axis=0, tiled=True),
    )
    acts_rot = lax.psum_scatter(
        jnp.dot(acts_feat, basis_in, preferred_element_type=jnp.float32),
        "tile",
        scatter_dimension=0,
        tiled=True,
    ).astype(jnp.bfloat16)
    grads_rot = lax.psum_scatter(
        jnp.dot(grads_feat, basis_out, preferred_element_type=jnp.float32),
        "tile",
        scatter_dimension=0,
        tiled=True,
    ).astype(jnp.bfloat16)
    grad_send = jnp.repeat(grads_rot.reshape(tok_rows, ROWB, tile_rows_n), col_blocks, axis=1)
    act_send = jnp.tile(acts_rot.reshape(tok_rows, col_blocks, tile_cols_n), (1, ROWB, 1))
    grad_tile, act_tile = (
        lax.all_to_all(grad_send, "tile", split_axis=1, concat_axis=0, tiled=True),
        lax.all_to_all(act_send, "tile", split_axis=1, concat_axis=0, tiled=True),
    )
    grad_tile = grad_tile.reshape(tok_rows * tiles, tile_rows_n)
    act_tile = act_tile.reshape(tok_rows * tiles, tile_cols_n)
    total_rows = grad_tile.shape[0]
    examples = total_rows // SEQ
    grad_ex = grad_tile.reshape(examples, SEQ, tile_rows_n)
    act_ex = act_tile.reshape(examples, SEQ, tile_cols_n)

    def accumulate(index, total):
        grad_part = grad_ex[index]
        act_part = act_ex[index]
        rotated = lax.dot_general(
            grad_part, act_part, (((0,), (0,)), ((), ())), preferred_element_type=jnp.float32
        )
        return total + rotated * rotated

    start = jnp.zeros((tile_rows_n, tile_cols_n), jnp.float32)
    total = lax.fori_loop(0, examples, accumulate, start)
    corr = total / float(examples * SEQ)
    return corr[None]


def solution(mesh):
    in_specs = (
        P(("grp", "tile"), None),
        P(("grp", "tile"), None),
        P("tile", None),
        P("tile", None),
    )
    out_specs = P(("grp", "tile"), None, None)
    return jax.shard_map(body, mesh=mesh, in_specs=in_specs, out_specs=out_specs, check_vma=False)
```

profile of v0, /device:TPU:0, one launch (start us, length us, event | category | flops | bytes accessed | tf_op | source)
XLA Modules:
  0.0 175.2 jit_solution(3713394253259764194)
XLA Ops:
  6.5 0.0 copy-start
  6.5 0.0 reduce-scatter.3.cloned.1.call-start
  6.5 14.4 %all_to_all.68 = bf16[8,16,256]{2,0,1:T(8,128)(2,1)S(1)} all-to-all(bf16[8,16,256]{2,0,1:T(8,128)(2,1)} %bitcast.43), channel_id=1, replica_groups=mesh['grp'=2,'tile'=16] {'tile'}, dimensions={1} | all-to-all | bytes 131072 | tf_op jit(solution)/shard_map/all_to_all | solution.py:20
  21.0 0.0 copy-done
  21.0 1.8 %fusion.8 = f32[128,4096]{1,0:T(8,128)} fusion(bf16[256,4096]{1,0:T(8,128)(2,1)S(1)} %copy-done, bf16[8,16,256]{2,0,1:T(8,128)(2,1)S(1)} %all_to_all.68), kind=kOutput, calls=%fused_computation.9 | convolution fusion | flops 268435456 | bytes 4259840 | tf_op jit(solution)/shard_map/dot_general | solution.py:29
  22.7 0.0 copy-start.1
  22.7 0.0 reduce-scatter.3.cloned.1.call-update
  22.8 0.0 reduce-scatter.5.cloned.1.call-start
  22.8 0.8 copy-done.1
  23.6 9.5 %all_to_all.69 = bf16[8,16,256]{2,0,1:T(8,128)(2,1)S(1)} all-to-all(bf16[8,16,256]{2,0,1:T(8,128)(2,1)S(1)} %bitcast.44), channel_id=1, replica_groups=mesh['grp'=2,'tile'=16] {'tile'}, dimensions={1} | all-to-all | bytes 131072 | tf_op jit(solution)/shard_map/all_to_all | solution.py:19
  33.0 3.4 %fusion.6 = f32[128,4096]{1,0:T(8,128)} fusion(bf16[256,4096]{1,0:T(8,128)(2,1)} %param.6, bf16[8,16,256]{2,0,1:T(8,128)(2,1)S(1)} %all_to_all.69), kind=kOutput, calls=%fused_computation.7 | convolution fusion | flops 268435456 | bytes 4259840 | tf_op jit(solution)/shard_map/dot_general | solution.py:23
  36.5 0.0 reduce-scatter.5.cloned.1.call-update
  36.5 45.3 %reduce-scatter.3.cloned.1.call-done = f32[8,4096]{1,0:T(8,128)} async-done(((f32[128,4096]{1,0:T(8,128)}), f32[8,4096]{1,0:T(8,128)}) %reduce-scatter.3.cloned.1.call-update) | async-done | bytes 131088 | tf_op jit(solution)/shard_map/reduce_scatter | solution.py:28
  81.8 0.9 convert_element_type.6
  82.7 0.7 broadcast_in_dim.7
  83.4 3.7 %all-to-all-start.1 = ((bf16[8,16,512]{2,0,1:T(8,128)(2,1)}), bf16[8,16,512]{2,0,1:T(8,128)(2,1)S(1)}, u32[]{:S(2)}, u32[]{:S(2)}) async-start(bf16[8,16,512]{2,0,1:T(8,128)(2,1)} %bitcast.4), calls=%async_computation.2 | async-start | bytes 262144 | tf_op jit(solution)/shard_map/all_to_all | solution.py:37
  87.1 59.5 %reduce-scatter.5.cloned.1.call-done = f32[8,4096]{1,0:T(8,128)} async-done(((f32[128,4096]{1,0:T(8,128)}), f32[8,4096]{1,0:T(8,128)}) %reduce-scatter.5.cloned.1.call-update) | async-done | bytes 131088 | tf_op jit(solution)/shard_map/reduce_scatter | solution.py:22
  146.6 0.9 convert_element_type.7
  147.5 0.0 all-to-all-done.1
  147.6 18.0 %all_to_all.70 = bf16[8,16,2048]{2,0,1:T(8,128)(2,1)S(1)} all-to-all(bf16[8,16,2048]{2,0,1:T(8,128)(2,1)S(1)} %bitcast.40), channel_id=1, replica_groups=mesh['grp'=2,'tile'=16] {'tile'}, dimensions={1} | all-to-all | bytes 1048576 | tf_op jit(solution)/shard_map/all_to_all | solution.py:38
  165.6 2.8 %fusion.1 = f32[1,512,2048]{2,1,0:T(8,128)} fusion(bf16[8,16,2048]{2,0,1:T(8,128)(2,1)S(1)} %all_to_all.70, bf16[8,16,512]{2,0,1:T(8,128)(2,1)S(1)} %all-to-all-done.1), kind=kOutput, calls=%fused_computation.2 | convolution fusion | flops 270532608 | bytes 4849664 | tf_op jit(solution)/shard_map/while/body/eval_jaxpr/dot_general | solution.py:50
  (1 shorter events, 0.0 us)
Async XLA Ops:
  6.5 14.4 %copy-start = (bf16[256,4096]{1,0:T(8,128)(2,1)S(1)}, bf16[256,4096]{1,0:T(8,128)(2,1)}, u32[]{:S(2)}) copy-start(bf16[256,4096]{1,0:T(8,128)(2,1)} %param.7) | copy-start | bytes 6291460
  6.5 75.3 %reduce-scatter.3.cloned.1.call-start = ((), (), s32[]{:S(2)}) async-start(), calls=%async_computation.6 | async-start | bytes 2228224 | tf_op jit(solution)/shard_map/reduce_scatter | solution.py:28
  22.7 0.8 copy-start.1
  22.8 123.9 %reduce-scatter.5.cloned.1.call-start = ((), (), s32[]{:S(2)}) async-start(), calls=%async_computation.7 | async-start | bytes 2228224 | tf_op jit(solution)/shard_map/reduce_scatter | solution.py:22
  83.4 64.1 %all-to-all-start.1 = ((bf16[8,16,512]{2,0,1:T(8,128)(2,1)}), bf16[8,16,512]{2,0,1:T(8,128)(2,1)S(1)}, u32[]{:S(2)}, u32[]{:S(2)}) async-start(bf16[8,16,512]{2,0,1:T(8,128)(2,1)} %bitcast.4), calls=%async_computation.2 | async-start | bytes 262144 | tf_op jit(solution)/shard_map/all_to_all | solution.py:37
Sparse Core Ops, SparseCore 0:
  22.9 58.9 reduce-scatter.2
  86.0 60.5 reduce-scatter.4
where the time goes:
time: 176 us; the launch traced here: 175 us
  waiting for transfers between devices  105 us (60%)
  blocking collectives  41.8 us (24%)
  between operations  13.4 us (8%)
  matrix products  8.01 us (5%)
  starting transfers between devices  3.77 us (2%)
  other arithmetic  1.82 us (1%)
    reduce_scatter x1, waiting for transfers between devices, body(): lax.psum_scatter(jnp.dot(acts_feat, basis_in, preferred_element_type=jnp....  59.5 us
    reduce_scatter x1, waiting for transfers between devices, body(): lax.psum_scatter(jnp.dot(grads_feat, basis_out, preferred_element_type=jn...  45.3 us
    all_to_all x1, blocking collectives, body(): lax.all_to_all(act_send, 'tile', split_axis=1, concat_axis=0, tiled=True)  18 us
    all_to_all x1, blocking collectives, body(): lax.all_to_all(grads, 'tile', split_axis=1, concat_axis=0, tiled=True)  14.4 us
    all_to_all x1, blocking collectives, body(): lax.all_to_all(acts, 'tile', split_axis=1, concat_axis=0, tiled=True)  9.47 us
    all_to_all x1, starting transfers between devices, body(): lax.all_to_all(grad_send, 'tile', split_axis=1, concat_axis=0, tiled=True)  3.73 us
  transfers between devices with their start and end apart: 3, of which 2 were waited for; matrix products, arithmetic and copies ran while one was open for 3% of the time, Pallas kernels for 0%

commit v1 on v0

--- a/solution.py
+++ b/solution.py
@@ -1,10 +1,308 @@
+import functools
+
 import jax
 import jax.numpy as jnp
 from jax import lax
+from jax.experimental import pallas as pl
+from jax.experimental.pallas import tpu as pltpu
 from jax.sharding import PartitionSpec as P
 
 SEQ = 128
 ROWB = 8
+CORES = 2
+YS = 2
+MESH = pl.DeviceIdType.MESH
+F32 = jnp.float32
+BF16 = jnp.bfloat16
+
+
+def rotate_kernel(
+    zs,
+    acts_ref, grads_ref, bin_hbm, bout_hbm,
+    aout_ref, gout_ref,
+    x, r, bi, bo,
+    ca_own, ca_send, ca_recv, cg_own, cg_send, cg_recv,
+    ya_send, ya_recv, yg_send, yg_recv,
+    za_send, za_recv, zg_send, zg_recv,
+    ag, gx,
+    basis_sem, tok_s, tok_r,
+    ca_s, ca_r, cg_s, cg_r,
+    ya_s, ya_r, yg_s, yg_r,
+    za_s, za_r, zg_s, zg_r,
+    agz_s, agz_r, agy_s, agy_r, gx_s, gx_r,
+):
+    n = CORES * YS * zs
+    tok = acts_ref.shape[0]
+    depth = bi.shape[0]
+    half_rows = gx.shape[1]
+    gcols = gx.shape[2]
+    acols = ag.shape[-1]
+    me = lax.axis_index("tile")
+    c = lax.rem(me, CORES)
+    y = lax.rem(me // CORES, YS)
+    z = me // (CORES * YS)
+    sib = me + 1 - 2 * c
+    yp = me + CORES * (1 - 2 * y)
+    oc, oy = 1 - c, 1 - y
+
+    def remote(src, dst, ssem, rsem, dev):
+        return pltpu.make_async_remote_copy(
+            src_ref=src, dst_ref=dst, send_sem=ssem, recv_sem=rsem,
+            device_id={"tile": dev}, device_id_type=MESH,
+        )
+
+    load_in = pltpu.make_async_copy(bin_hbm, bi, basis_sem.at[0])
+    load_out = pltpu.make_async_copy(bout_hbm, bo, basis_sem.at[1])
+    load_out.start()
+    load_in.start()
+
+    barrier = pltpu.get_barrier_semaphore()
+
+    def greet(i, carry):
+        pl.semaphore_signal(
+            barrier, inc=1, device_id={"tile": lax.rem(me + i, n)}, device_id_type=MESH
+        )
+        return carry
+
+    lax.fori_loop(1, n, greet, 0)
+    x[...] = jnp.concatenate(
+        [acts_ref[...].astype(F32), grads_ref[...].astype(F32)], axis=0
+    ).astype(BF16)
+    pl.semaphore_wait(barrier, n - 1)
+
+    def tok_copy(to, frm):
+        return remote(
+            x.at[:, pl.ds(pl.multiple_of(to * depth, depth), depth)],
+            r.at[frm], tok_s.at[to], tok_r.at[frm], to,
+        )
+
+    def send_tok(i, carry):
+        tok_copy(lax.rem(me + i, n), me).start()
+        return carry
+
+    lax.fori_loop(1, n, send_tok, 0)
+    r[pl.ds(me, 1)] = x[:, pl.ds(pl.multiple_of(me * depth, depth), depth)][None]
+
+    def recv_tok(i, carry):
+        tok_copy(me, lax.rem(me + n - i, n)).wait_recv()
+        return carry
+
+    lax.fori_loop(1, n, recv_tok, 0)
+    both = r[...].astype(F32)
+    a = both[:, :tok].reshape(n * tok, depth).astype(BF16)
+    g = both[:, tok:].reshape(n * tok, depth).astype(BF16)
+    load_out.wait()
+    load_in.wait()
+
+
+    def core_a(yy, zz):
+        return remote(
+            ca_send.at[yy, zz], ca_recv.at[yy, zz], ca_s.at[yy, zz], ca_r.at[yy, zz], sib
+        )
+
+    def core_g(yy, zz):
+        return remote(
+            cg_send.at[yy, zz], cg_recv.at[yy, zz], cg_s.at[yy, zz], cg_r.at[yy, zz], sib
+        )
+
+    def acol(cc, yy, zz):
+        start = ((cc * YS + yy) * zs + zz) * acols
+        return pl.ds(pl.multiple_of(start, acols), acols)
+
+    def make_chunk(yy, zz):
+        ca_send[yy, zz] = jnp.dot(a, bi[:, acol(oc, yy, zz)], preferred_element_type=F32)
+        core_a(yy, zz).start()
+        gpart = jnp.dot(
+            g,
+            bo[:, pl.ds(pl.multiple_of((zz * YS + yy) * gcols, gcols), gcols)],
+            preferred_element_type=F32,
+        )
+        low, high = gpart[:half_rows], gpart[half_rows:]
+        cg_send[yy, zz] = jnp.where(c == 0, high, low)
+        core_g(yy, zz).start()
+        cg_own[yy, zz] = jnp.where(c == 0, low, high)
+        ca_own[yy, zz] = jnp.dot(a, bi[:, acol(c, yy, zz)], preferred_element_type=F32)
+
+    def y_a(zz):
+        return remote(ya_send.at[zz], ya_recv.at[zz], ya_s.at[zz], ya_r.at[zz], yp)
+
+    def y_g(zz):
+        return remote(yg_send.at[zz], yg_recv.at[zz], yg_s.at[zz], yg_r.at[zz], yp)
+
+    def zdev(zz):
+        return zz * (CORES * YS) + lax.rem(me, CORES * YS)
+
+    def z_a(to, frm):
+        return remote(za_send.at[to], za_recv.at[frm], za_s.at[to], za_r.at[frm], zdev(to))
+
+    def z_g(to, frm):
+        return remote(zg_send.at[to], zg_recv.at[frm], zg_s.at[to], zg_r.at[frm], zdev(to))
+
+    order = [lax.rem(z + 1 + i, zs) for i in range(zs)]
+
+    for zz in order:
+        make_chunk(oy, zz)
+    for zz in order:
+        core_a(oy, zz).wait_recv()
+        ya_send[zz] = (ca_own[oy, zz] + ca_recv[oy, zz]).astype(BF16)
+        y_a(zz).start()
+        core_g(oy, zz).wait_recv()
+        yg_send[zz] = (cg_own[oy, zz] + cg_recv[oy, zz]).astype(BF16)
+        y_g(zz).start()
+        make_chunk(y, zz)
+    for i, zz in enumerate(order):
+        core_a(y, zz).wait_recv()
+        y_a(zz).wait_recv()
+        total = ca_own[y, zz] + ca_recv[y, zz] + ya_recv[zz].astype(F32)
+        if i < zs - 1:
+            za_send[zz] = total.astype(BF16)
+            z_a(zz, z).start()
+        else:
+            ca_own[y, zz] = total
+        core_g(y, zz).wait_recv()
+        y_g(zz).wait_recv()
+        total = cg_own[y, zz] + cg_recv[y, zz] + yg_recv[zz].astype(F32)
+        if i < zs - 1:
+            zg_send[zz] = total.astype(BF16)
+            z_g(zz, z).start()
+        else:
+            cg_own[y, zz] = total
+
+    others = [lax.rem(z + zs - 1 - i, zs) for i in range(zs - 1)]
+    total = ca_own[y, z]
+    for zz in others:
+        z_a(z, zz).wait_recv()
+        total = total + za_recv[zz].astype(F32)
+    ag[y, z] = total.astype(BF16)
+
+    def ag_z(to, frm):
+        return remote(ag.at[y, frm], ag.at[y, frm], agz_s.at[to], agz_r.at[frm], zdev(to))
+
+    def ag_y(yy, zz):
+        return remote(ag.at[yy, zz], ag.at[yy, zz], agy_s.at[zz], agy_r.at[zz], yp)
+
+    for zz in order[:-1]:
+        ag_z(zz, z).start()
+    ag_y(y, z).start()
+
+    total = cg_own[y, z]
+    for zz in others:
+        z_g(z, zz).wait_recv()
+        total = total + zg_recv[zz].astype(F32)
+    gx[c] = total
+    swap = remote(gx.at[c], gx.at[c], gx_s, gx_r, sib)
+    swap.start()
+
+    for zz in others:
+        ag_z(z, zz).wait_recv()
+        ag_y(y, zz).start()
+    aout_ref[y] = ag[y]
+    remote(gx.at[oc], gx.at[oc], gx_s, gx_r, sib).wait_recv()
+    gout_ref[...] = gx[...]
+    for zz in [z] + others:
+        ag_y(oy, zz).wait_recv()
+        aout_ref[oy, zz] = ag[oy, zz]
+
+    def sent_tok(i, carry):
+        tok_copy(lax.rem(me + i, n), me).wait_send()
+        return carry
+
+    lax.fori_loop(1, n, sent_tok, 0)
+    for zz in order:
+        core_a(oy, zz).wait_send()
+        core_g(oy, zz).wait_send()
+        core_a(y, zz).wait_send()
+        core_g(y, zz).wait_send()
+        y_a(zz).wait_send()
+        y_g(zz).wait_send()
+        ag_y(y, zz).wait_send()
+    for zz in order[:-1]:
+        z_a(zz, z).wait_send()
+        z_g(zz, z).wait_send()
+        ag_z(zz, z).wait_send()
+    swap.wait_send()
+
+
+def rotate(acts, grads, basis_in, basis_out, tiles):
+    zs = tiles // (CORES * YS)
+    tok, width_in = acts.shape
+    width_out = grads.shape[1]
+    depth = basis_in.shape[0]
+    tokens = tok * tiles
+    half = tokens // CORES
+    acols = width_in // tiles
+    gcols = width_out // ROWB
+    a_grid, g_grid = (YS, zs, tokens, acols), (YS, zs, half, gcols)
+    dma = pltpu.SemaphoreType.DMA
+    scratch = [
+        pltpu.VMEM((2 * tok, width_in), BF16),
+        pltpu.VMEM((tiles, 2 * tok, depth), BF16),
+        pltpu.VMEM((depth, width_in), BF16),
+        pltpu.VMEM((depth, width_out), BF16),
+    ]
+    scratch += [pltpu.VMEM(a_grid, F32)] * 3 + [pltpu.VMEM(g_grid, F32)] * 3
+    for _ in range(2):
+        scratch += [pltpu.VMEM(a_grid[1:], BF16)] * 2 + [pltpu.VMEM(g_grid[1:], BF16)] * 2
+    scratch += [pltpu.VMEM(a_grid, BF16), pltpu.VMEM((CORES, half, gcols), F32)]
+    scratch += [dma((2,)), dma((tiles,)), dma((tiles,))]
+    scratch += [dma((YS, zs))] * 4 + [dma((zs,))] * 12 + [dma, dma]
+    return pl.pallas_call(
+        functools.partial(rotate_kernel, zs),
+        out_shape=(
+            jax.ShapeDtypeStruct(a_grid, BF16),
+            jax.ShapeDtypeStruct((CORES, half, gcols), F32),
+        ),
+        in_specs=[pl.BlockSpec(memory_space=pltpu.VMEM)] * 2
+        + [pl.BlockSpec(memory_space=pl.ANY)] * 2,
+        out_specs=(pl.BlockSpec(memory_space=pltpu.VMEM),) * 2,
+        scratch_shapes=scratch,
+        compiler_params=pltpu.CompilerParams(
+            collective_id=0, has_side_effects=True, vmem_limit_bytes=40 * 1024 * 1024
+        ),
+        name="rotate",
+    )(acts, grads, basis_in, basis_out)
+
+
+def correct_kernel(scale, a_ref, g_ref, out_ref, lhs):
+    tokens = g_ref.shape[0]
+
+    @pl.when(pl.program_id(0) == 0)
+    def _():
+        gt = g_ref[...].T
+        high = gt.astype(BF16)
+        lhs[:, :tokens] = high
+        lhs[:, tokens:] = (gt - high.astype(F32)).astype(BF16)
+
+    a = a_ref[0]
+    rotated = jnp.dot(
+        lhs[...], jnp.concatenate([a, a], axis=0), preferred_element_type=F32
+    )
+    out_ref[0] = rotated * rotated * scale
+
+
+def correct(a, g):
+    blocks, tokens, acols = a.shape
+    rows = g.shape[1]
+    return pl.pallas_call(
+        functools.partial(correct_kernel, 1.0 / tokens),
+        grid=(blocks,),
+        out_shape=jax.ShapeDtypeStruct((1, rows, blocks * acols), F32),
+        in_specs=[
+            pl.BlockSpec((1, tokens, acols), lambda i: (i, 0, 0)),
+            pl.BlockSpec((tokens, rows), lambda i: (0, 0)),
+        ],
+        out_specs=pl.BlockSpec((1, rows, acols), lambda i: (0, 0, i)),
+        scratch_shapes=[pltpu.VMEM((rows, 2 * tokens), BF16)],
+        compiler_params=pltpu.CompilerParams(vmem_limit_bytes=16 * 1024 * 1024),
+        name="correct",
+    )(a, g)
+
+
+def chip_body(acts, grads, basis_in, basis_out):
+    tiles = lax.axis_size("tile")
+    a, g = rotate(acts, grads, basis_in, basis_out, tiles)
+    tokens = a.shape[2]
+    return correct(a.reshape(-1, tokens, a.shape[3]), g.reshape(tokens, g.shape[2]))
 
 
 def body(acts, grads, basis_in, basis_out):
@@ -66,4 +364,14 @@
         P("tile", None),
     )
     out_specs = P(("grp", "tile"), None, None)
-    return jax.shard_map(body, mesh=mesh, in_specs=in_specs, out_specs=out_specs, check_vma=False)
+
+    def whole(acts, grads, basis_in, basis_out):
+        tiles = mesh.shape["tile"]
+        tokens = acts.shape[0] // mesh.shape["grp"]
+        per_chip = tiles == CORES * ROWB and tokens == SEQ
+        return jax.shard_map(
+            chip_body if per_chip else body,
+            mesh=mesh, in_specs=in_specs, out_specs=out_specs, check_vma=False,
+        )(acts, grads, basis_in, basis_out)
+
+    return whole

time: 176 us -> 50.3 us (0.29)
  waiting for transfers between devices: 105 us -> 0 us
  Pallas kernels: 0 us -> 45.2 us
  blocking collectives: 41.8 us -> 0 us
  between operations: 13.4 us -> 0.01 us
  matrix products: 8.01 us -> 0 us
  starting transfers between devices: 3.77 us -> 0 us
  local copies, waits for them, and re-layouts: 1.47 us -> 4.86 us
  other arithmetic: 1.82 us -> 0 us
    reduce_scatter x2 -> x0, waiting for transfers between devices: 105 us -> none  [the longest x1 59.5 us: body(): lax.psum_scatter(jnp.dot(acts_feat, basis_in, preferred_element_type=jnp....]
    pallas_call x0 -> x2, Pallas kernels: none -> 45.2 us  [the longest x1 40.7 us: rotate(): pl.pallas_call(functools.partial(rotate_kernel, zs), out_shape=(jax.Shape...]
    all_to_all x3 -> x0, blocking collectives: 41.8 us -> none  [the longest x1 18 us: body(): lax.all_to_all(act_send, 'tile', split_axis=1, concat_axis=0, tiled=True)]
    dot_general x3 -> x0, matrix products: 8.01 us -> none  [the longest x1 3.43 us: body(): jnp.dot(acts_feat, basis_in, preferred_element_type=jnp.float32)]
    unnamed x4 -> x8, local copies, waits for them, and re-layouts: 0.77 us -> 4.86 us
    all_to_all x1 -> x0, starting transfers between devices: 3.73 us -> none  [body(): lax.all_to_all(grad_send, 'tile', split_axis=1, concat_axis=0, tiled=True)]
    convert_element_type x2 -> x0, other arithmetic: 1.82 us -> none  [the longest x1 0.91 us: body(): grads_rot = lax.psum_scatter(jnp.dot(grads_feat, basis_out, preferred_ele...]
  transfers between devices with their start and end apart: 3 -> 0, of which waited for: 2 -> 0; matrix products, arithmetic and copies ran while one was open for 3% -> 0% of each run, Pallas kernels for 0% -> 0%
where the time goes in v1:
time: 50.3 us; the launch traced here: 50.1 us
  Pallas kernels  45.2 us (90%)
  local copies, waits for them, and re-layouts  4.86 us (10%)
    pallas_call x1, Pallas kernels, rotate(): pl.pallas_call(functools.partial(rotate_kernel, zs), out_shape=(jax.Shape...  40.7 us
    unnamed x8, local copies, waits for them, and re-layouts  4.86 us
    pallas_call x1, Pallas kernels, correct(): pl.pallas_call(functools.partial(correct_kernel, 1.0 / tokens), grid=(blo...  4.5 us

profile of v1, /device:TPU:0, one launch (start us, length us, event | category | flops | bytes accessed | tf_op | source)
XLA Modules:
  0.0 50.1 jit_solution(4167512357735370219)
XLA Ops:
  0.0 0.0 copy-start
  0.0 1.6 %copy-done = bf16[256,4096]{1,0:T(8,128)(2,1)S(1)} copy-done((bf16[256,4096]{1,0:T(8,128)(2,1)S(1)}, bf16[256,4096]{1,0:T(8,128)(2,1)}, u32[]{:S(2)}) %copy-start) | copy-done | bytes 2097176
  1.6 0.0 copy-start.1
  1.6 1.6 %copy-done.1 = bf16[256,4096]{1,0:T(8,128)(2,1)S(1)} copy-done((bf16[256,4096]{1,0:T(8,128)(2,1)S(1)}, bf16[256,4096]{1,0:T(8,128)(2,1)}, u32[]{:S(2)}) %copy-start.1) | copy-done | bytes 2097176
  3.2 0.0 copy-start.2
  3.2 0.8 %copy-done.2 = bf16[8,4096]{1,0:T(8,128)(2,1)S(1)} copy-done((bf16[8,4096]{1,0:T(8,128)(2,1)S(1)}, bf16[8,4096]{1,0:T(8,128)(2,1)}, u32[]{:S(2)}) %copy-start.2) | copy-done | bytes 65560
  4.0 0.0 copy-start.3
  4.0 0.8 %copy-done.3 = bf16[8,4096]{1,0:T(8,128)(2,1)S(1)} copy-done((bf16[8,4096]{1,0:T(8,128)(2,1)S(1)}, bf16[8,4096]{1,0:T(8,128)(2,1)}, u32[]{:S(2)}) %copy-start.3) | copy-done | bytes 65560
  4.9 40.7 %rotate.1 = (bf16[2,4,128,256]{3,2,1,0:T(8,128)(2,1)S(1)}, f32[2,64,512]{2,1,0:T(8,128)S(1)}) custom-call(bf16[8,4096]{1,0:T(8,128)(2,1)S(1)} %copy-done.2, bf16[8,4096]{1,0:T(8,128)(2,1)S(1)} %copy-done.3, bf16[256,4096]{1,0:T(8,128)(2,1)S(1)} %copy-done, bf16[256,4096]{1,0:T(8,128)(2,1)S(1)} %copy-done.1), custom_call_target="tpu_custom_call" | custom-call | tf_op jit(solution)/shard_map/rotate/pallas_call | solution.py:249
  45.6 4.5 %correct.1 = f32[1,512,2048]{2,1,0:T(8,128)} custom-call(bf16[8,128,256]{2,1,0:T(8,128)(2,1)S(1)} %bitcast.2, f32[128,512]{1,0:T(8,128)S(1)} %bitcast.3), custom_call_target="tpu_custom_call" | custom-call | tf_op jit(solution)/shard_map/correct/pallas_call | solution.py:286
Async XLA Ops:
  0.0 1.6 %copy-start = (bf16[256,4096]{1,0:T(8,128)(2,1)S(1)}, bf16[256,4096]{1,0:T(8,128)(2,1)}, u32[]{:S(2)}) copy-start(bf16[256,4096]{1,0:T(8,128)(2,1)} %bin_hbm.1) | copy-start | bytes 6291460
  1.6 1.6 %copy-start.1 = (bf16[256,4096]{1,0:T(8,128)(2,1)S(1)}, bf16[256,4096]{1,0:T(8,128)(2,1)}, u32[]{:S(2)}) copy-start(bf16[256,4096]{1,0:T(8,128)(2,1)} %bout_hbm.1) | copy-start | bytes 6291460
  3.2 0.8 %copy-start.2 = (bf16[8,4096]{1,0:T(8,128)(2,1)S(1)}, bf16[8,4096]{1,0:T(8,128)(2,1)}, u32[]{:S(2)}) copy-start(bf16[8,4096]{1,0:T(8,128)(2,1)} %acts_ref.1) | copy-start | bytes 196612
  4.0 0.8 %copy-start.3 = (bf16[8,4096]{1,0:T(8,128)(2,1)S(1)}, bf16[8,4096]{1,0:T(8,128)(2,1)}, u32[]{:S(2)}) copy-start(bf16[8,4096]{1,0:T(8,128)(2,1)} %grads_ref.1) | copy-start | bytes 196612

commit v2 on v1

--- a/solution.py
+++ b/solution.py
@@ -12,15 +12,16 @@
 CORES = 2
 YS = 2
 MESH = pl.DeviceIdType.MESH
+VMEM_LIMIT = 62 * 1024 * 1024
 F32 = jnp.float32
 BF16 = jnp.bfloat16
 
 
 def rotate_kernel(
     zs,
-    acts_ref, grads_ref, bin_hbm, bout_hbm,
+    acts_hbm, grads_hbm, bin_hbm, bout_hbm,
     aout_ref, gout_ref,
-    x, r, bi, bo,
+    acts_ref, grads_ref, x, r, bi, bo,
     ca_own, ca_send, ca_recv, cg_own, cg_send, cg_recv,
     ya_send, ya_recv, yg_send, yg_recv,
     za_send, za_recv, zg_send, zg_recv,
@@ -53,8 +54,12 @@
 
     load_in = pltpu.make_async_copy(bin_hbm, bi, basis_sem.at[0])
     load_out = pltpu.make_async_copy(bout_hbm, bo, basis_sem.at[1])
+    load_a = pltpu.make_async_copy(acts_hbm, acts_ref, basis_sem.at[2])
+    load_g = pltpu.make_async_copy(grads_hbm, grads_ref, basis_sem.at[3])
+    load_a.start()
+    load_g.start()
+    load_in.start()
     load_out.start()
-    load_in.start()
 
     barrier = pltpu.get_barrier_semaphore()
 
@@ -65,6 +70,8 @@
         return carry
 
     lax.fori_loop(1, n, greet, 0)
+    load_a.wait()
+    load_g.wait()
     x[...] = jnp.concatenate(
         [acts_ref[...].astype(F32), grads_ref[...].astype(F32)], axis=0
     ).astype(BF16)
@@ -109,9 +116,14 @@
         start = ((cc * YS + yy) * zs + zz) * acols
         return pl.ds(pl.multiple_of(start, acols), acols)
 
-    def make_chunk(yy, zz):
+    def send_a(yy, zz):
         ca_send[yy, zz] = jnp.dot(a, bi[:, acol(oc, yy, zz)], preferred_element_type=F32)
         core_a(yy, zz).start()
+
+    def keep_a(yy, zz):
+        ca_own[yy, zz] = jnp.dot(a, bi[:, acol(c, yy, zz)], preferred_element_type=F32)
+
+    def make_g(yy, zz):
         gpart = jnp.dot(
             g,
             bo[:, pl.ds(pl.multiple_of((zz * YS + yy) * gcols, gcols), gcols)],
@@ -121,7 +133,6 @@
         cg_send[yy, zz] = jnp.where(c == 0, high, low)
         core_g(yy, zz).start()
         cg_own[yy, zz] = jnp.where(c == 0, low, high)
-        ca_own[yy, zz] = jnp.dot(a, bi[:, acol(c, yy, zz)], preferred_element_type=F32)
 
     def y_a(zz):
         return remote(ya_send.at[zz], ya_recv.at[zz], ya_s.at[zz], ya_r.at[zz], yp)
@@ -140,16 +151,20 @@
 
     order = [lax.rem(z + 1 + i, zs) for i in range(zs)]
 
-    for zz in order:
-        make_chunk(oy, zz)
-    for zz in order:
+    others = [lax.rem(z + zs - 1 - i, zs) for i in range(zs - 1)]
+
+    for zz in order:
+        send_a(oy, zz)
+    for zz in order:
+        keep_a(oy, zz)
         core_a(oy, zz).wait_recv()
         ya_send[zz] = (ca_own[oy, zz] + ca_recv[oy, zz]).astype(BF16)
         y_a(zz).start()
-        core_g(oy, zz).wait_recv()
-        yg_send[zz] = (cg_own[oy, zz] + cg_recv[oy, zz]).astype(BF16)
-        y_g(zz).start()
-        make_chunk(y, zz)
+    for zz in order:
+        send_a(y, zz)
+        keep_a(y, zz)
+    for zz in order:
+        make_g(oy, zz)
     for i, zz in enumerate(order):
         core_a(y, zz).wait_recv()
         y_a(zz).wait_recv()
@@ -159,6 +174,29 @@
             z_a(zz, z).start()
         else:
             ca_own[y, zz] = total
+        core_g(oy, zz).wait_recv()
+        yg_send[zz] = (cg_own[oy, zz] + cg_recv[oy, zz]).astype(BF16)
+        y_g(zz).start()
+        make_g(y, zz)
+
+    total = ca_own[y, z]
+    for zz in others:
+        z_a(z, zz).wait_recv()
+        total = total + za_recv[zz].astype(F32)
+    ag[y, z] = total.astype(BF16)
+
+    def ag_z(to, frm):
+        return remote(ag.at[y, frm], ag.at[y, frm], agz_s.at[to], agz_r.at[frm], zdev(to))
+
+    def ag_y(yy, zz):
+        return remote(ag.at[yy, zz], ag.at[yy, zz], agy_s.at[zz], agy_r.at[zz], yp)
+
+    for zz in order[:-1]:
+        ag_z(zz, z).start()
+    ag_y(y, z).start()
+
+    def finish_g(i):
+        zz = order[i]
         core_g(y, zz).wait_recv()
         y_g(zz).wait_recv()
         total = cg_own[y, zz] + cg_recv[y, zz] + yg_recv[zz].astype(F32)
@@ -168,22 +206,12 @@
         else:
             cg_own[y, zz] = total
 
-    others = [lax.rem(z + zs - 1 - i, zs) for i in range(zs - 1)]
-    total = ca_own[y, z]
+    for i in range(zs - 1):
+        finish_g(i)
     for zz in others:
-        z_a(z, zz).wait_recv()
-        total = total + za_recv[zz].astype(F32)
-    ag[y, z] = total.astype(BF16)
-
-    def ag_z(to, frm):
-        return remote(ag.at[y, frm], ag.at[y, frm], agz_s.at[to], agz_r.at[frm], zdev(to))
-
-    def ag_y(yy, zz):
-        return remote(ag.at[yy, zz], ag.at[yy, zz], agy_s.at[zz], agy_r.at[zz], yp)
-
-    for zz in order[:-1]:
-        ag_z(zz, z).start()
-    ag_y(y, z).start()
+        ag_z(z, zz).wait_recv()
+        ag_y(y, zz).start()
+    finish_g(zs - 1)
 
     total = cg_own[y, z]
     for zz in others:
@@ -192,13 +220,12 @@
     gx[c] = total
     swap = remote(gx.at[c], gx.at[c], gx_s, gx_r, sib)
     swap.start()
-
-    for zz in others:
-        ag_z(z, zz).wait_recv()
-        ag_y(y, zz).start()
     aout_ref[y] = ag[y]
     remote(gx.at[oc], gx.at[oc], gx_s, gx_r, sib).wait_recv()
-    gout_ref[...] = gx[...]
+    gt = gx[...].reshape(CORES * half_rows, gcols).T
+    high = gt.astype(BF16)
+    gout_ref[:, : CORES * half_rows] = high
+    gout_ref[:, CORES * half_rows :] = (gt - high.astype(F32)).astype(BF16)
     for zz in [z] + others:
         ag_y(oy, zz).wait_recv()
         aout_ref[oy, zz] = ag[oy, zz]
@@ -234,7 +261,8 @@
     gcols = width_out // ROWB
     a_grid, g_grid = (YS, zs, tokens, acols), (YS, zs, half, gcols)
     dma = pltpu.SemaphoreType.DMA
-    scratch = [
+    scratch = [pltpu.VMEM(acts.shape, BF16), pltpu.VMEM(grads.shape, BF16)]
+    scratch += [
         pltpu.VMEM((2 * tok, width_in), BF16),
         pltpu.VMEM((tiles, 2 * tok, depth), BF16),
         pltpu.VMEM((depth, width_in), BF16),
@@ -244,56 +272,48 @@
     for _ in range(2):
         scratch += [pltpu.VMEM(a_grid[1:], BF16)] * 2 + [pltpu.VMEM(g_grid[1:], BF16)] * 2
     scratch += [pltpu.VMEM(a_grid, BF16), pltpu.VMEM((CORES, half, gcols), F32)]
-    scratch += [dma((2,)), dma((tiles,)), dma((tiles,))]
+    scratch += [dma((4,)), dma((tiles,)), dma((tiles,))]
     scratch += [dma((YS, zs))] * 4 + [dma((zs,))] * 12 + [dma, dma]
     return pl.pallas_call(
         functools.partial(rotate_kernel, zs),
         out_shape=(
             jax.ShapeDtypeStruct(a_grid, BF16),
-            jax.ShapeDtypeStruct((CORES, half, gcols), F32),
+            jax.ShapeDtypeStruct((gcols, 2 * tokens), BF16),
         ),
-        in_specs=[pl.BlockSpec(memory_space=pltpu.VMEM)] * 2
-        + [pl.BlockSpec(memory_space=pl.ANY)] * 2,
+        in_specs=[pl.BlockSpec(memory_space=pl.ANY)] * 4,
         out_specs=(pl.BlockSpec(memory_space=pltpu.VMEM),) * 2,
         scratch_shapes=scratch,
         compiler_params=pltpu.CompilerParams(
-            collective_id=0, has_side_effects=True, vmem_limit_bytes=40 * 1024 * 1024
+            collective_id=0, has_side_effects=True, vmem_limit_bytes=VMEM_LIMIT
         ),
         name="rotate",
     )(acts, grads, basis_in, basis_out)
 
 
-def correct_kernel(scale, a_ref, g_ref, out_ref, lhs):
-    tokens = g_ref.shape[0]
-
-    @pl.when(pl.program_id(0) == 0)
-    def _():
-        gt = g_ref[...].T
-        high = gt.astype(BF16)
-        lhs[:, :tokens] = high
-        lhs[:, tokens:] = (gt - high.astype(F32)).astype(BF16)
-
-    a = a_ref[0]
-    rotated = jnp.dot(
-        lhs[...], jnp.concatenate([a, a], axis=0), preferred_element_type=F32
-    )
-    out_ref[0] = rotated * rotated * scale
+def correct_kernel(scale, a_ref, g_ref, out_ref):
+    acols = a_ref.shape[2]
+    for k in range(a_ref.shape[0]):
+        a = a_ref[k]
+        rotated = jnp.dot(
+            g_ref[...], jnp.concatenate([a, a], axis=0), preferred_element_type=F32
+        )
+        out_ref[0, :, k * acols : (k + 1) * acols] = rotated * rotated * scale
 
 
 def correct(a, g):
     blocks, tokens, acols = a.shape
-    rows = g.shape[1]
+    rows = g.shape[0]
+    step = 2
     return pl.pallas_call(
         functools.partial(correct_kernel, 1.0 / tokens),
-        grid=(blocks,),
+        grid=(blocks // step,),
         out_shape=jax.ShapeDtypeStruct((1, rows, blocks * acols), F32),
         in_specs=[
-            pl.BlockSpec((1, tokens, acols), lambda i: (i, 0, 0)),
-            pl.BlockSpec((tokens, rows), lambda i: (0, 0)),
+            pl.BlockSpec((step, tokens, acols), lambda i: (i, 0, 0)),
+            pl.BlockSpec((rows, 2 * tokens), lambda i: (0, 0)),
         ],
-        out_specs=pl.BlockSpec((1, rows, acols), lambda i: (0, 0, i)),
-        scratch_shapes=[pltpu.VMEM((rows, 2 * tokens), BF16)],
-        compiler_params=pltpu.CompilerParams(vmem_limit_bytes=16 * 1024 * 1024),
+        out_specs=pl.BlockSpec((1, rows, step * acols), lambda i: (0, 0, i)),
+        compiler_params=pltpu.CompilerParams(vmem_limit_bytes=VMEM_LIMIT),
         name="correct",
     )(a, g)
 
@@ -302,7 +322,7 @@
     tiles = lax.axis_size("tile")
     a, g = rotate(acts, grads, basis_in, basis_out, tiles)
     tokens = a.shape[2]
-    return correct(a.reshape(-1, tokens, a.shape[3]), g.reshape(tokens, g.shape[2]))
+    return correct(a.reshape(-1, tokens, a.shape[3]), g)
 
 
 def body(acts, grads, basis_in, basis_out):

time: 50.3 us -> 42.9 us (0.85)
  local copies, waits for them, and re-layouts: 4.86 us -> 0 us
  Pallas kernels: 45.2 us -> 42.4 us
    unnamed x8 -> x0, local copies, waits for them, and re-layouts: 4.86 us -> none
    pallas_call x1, Pallas kernels: 40.7 us -> 37.9 us  [rotate(): pl.pallas_call(functools.partial(rotate_kernel, zs), out_shape=(jax.Shape...]
where the time goes in v2:
time: 42.9 us; the launch traced here: 42.4 us
  Pallas kernels  42.4 us (99%)
    pallas_call x1, Pallas kernels, rotate(): pl.pallas_call(functools.partial(rotate_kernel, zs), out_shape=(jax.Shape...  37.9 us
    pallas_call x1, Pallas kernels, correct(): pl.pallas_call(functools.partial(correct_kernel, 1.0 / tokens), grid=(blo...  4.49 us

profile of v2, /device:TPU:0, one launch (start us, length us, event | category | flops | bytes accessed | tf_op | source)
XLA Modules:
  0.0 42.4 jit_solution(15322971351780233223)
XLA Ops:
  0.0 37.9 %rotate.1 = (bf16[2,4,128,256]{3,2,1,0:T(8,128)(2,1)}, bf16[512,256]{1,0:T(8,128)(2,1)}) custom-call(bf16[8,4096]{1,0:T(8,128)(2,1)} %acts_hbm.1, bf16[8,4096]{1,0:T(8,128)(2,1)} %grads_hbm.1, bf16[256,4096]{1,0:T(8,128)(2,1)} %bin_hbm.1, bf16[256,4096]{1,0:T(8,128)(2,1)} %bout_hbm.1), custom_call_target="tpu_custom_call" | custom-call | tf_op jit(solution)/shard_map/rotate/pallas_call | solution.py:277
  37.9 4.5 %correct.1 = f32[1,512,2048]{2,1,0:T(8,128)} custom-call(bf16[8,128,256]{2,1,0:T(8,128)(2,1)} %bitcast.1, bf16[512,256]{1,0:T(8,128)(2,1)} %get-tuple-element.8.g_ref), custom_call_target="tpu_custom_call" | custom-call | tf_op jit(solution)/shard_map/correct/pallas_call | solution.py:307

commit v3 on v2

--- a/solution.py
+++ b/solution.py
@@ -12,16 +12,16 @@
 CORES = 2
 YS = 2
 MESH = pl.DeviceIdType.MESH
-VMEM_LIMIT = 62 * 1024 * 1024
+VMEM_LIMIT = 52 * 1024 * 1024
 F32 = jnp.float32
 BF16 = jnp.bfloat16
 
 
 def rotate_kernel(
     zs,
-    acts_hbm, grads_hbm, bin_hbm, bout_hbm,
+    x, bin_hbm, bout_hbm,
     aout_ref, gout_ref,
-    acts_ref, grads_ref, x, r, bi, bo,
+    r, bi, bo,
     ca_own, ca_send, ca_recv, cg_own, cg_send, cg_recv,
     ya_send, ya_recv, yg_send, yg_recv,
     za_send, za_recv, zg_send, zg_recv,
@@ -33,7 +33,7 @@
     agz_s, agz_r, agy_s, agy_r, gx_s, gx_r,
 ):
     n = CORES * YS * zs
-    tok = acts_ref.shape[0]
+    tok = x.shape[0] // 2
     depth = bi.shape[0]
     half_rows = gx.shape[1]
     gcols = gx.shape[2]
@@ -54,10 +54,6 @@
 
     load_in = pltpu.make_async_copy(bin_hbm, bi, basis_sem.at[0])
     load_out = pltpu.make_async_copy(bout_hbm, bo, basis_sem.at[1])
-    load_a = pltpu.make_async_copy(acts_hbm, acts_ref, basis_sem.at[2])
-    load_g = pltpu.make_async_copy(grads_hbm, grads_ref, basis_sem.at[3])
-    load_a.start()
-    load_g.start()
     load_in.start()
     load_out.start()
 
@@ -70,11 +66,6 @@
         return carry
 
     lax.fori_loop(1, n, greet, 0)
-    load_a.wait()
-    load_g.wait()
-    x[...] = jnp.concatenate(
-        [acts_ref[...].astype(F32), grads_ref[...].astype(F32)], axis=0
-    ).astype(BF16)
     pl.semaphore_wait(barrier, n - 1)
 
     def tok_copy(to, frm):
@@ -134,8 +125,13 @@
         core_g(yy, zz).start()
         cg_own[yy, zz] = jnp.where(c == 0, low, high)
 
-    def y_a(zz):
-        return remote(ya_send.at[zz], ya_recv.at[zz], ya_s.at[zz], ya_r.at[zz], yp)
+    def rows(h):
+        return pl.ds(h * half_rows, half_rows)
+
+    def y_a(h, zz):
+        return remote(
+            ya_send.at[zz, rows(h)], ya_recv.at[zz, rows(h)], ya_s.at[h, zz], ya_r.at[h, zz], yp
+        )
 
     def y_g(zz):
         return remote(yg_send.at[zz], yg_recv.at[zz], yg_s.at[zz], yg_r.at[zz], yp)
@@ -143,8 +139,11 @@
     def zdev(zz):
         return zz * (CORES * YS) + lax.rem(me, CORES * YS)
 
-    def z_a(to, frm):
-        return remote(za_send.at[to], za_recv.at[frm], za_s.at[to], za_r.at[frm], zdev(to))
+    def z_a(h, to, frm):
+        return remote(
+            za_send.at[to, rows(h)], za_recv.at[frm, rows(h)],
+            za_s.at[h, to], za_r.at[h, frm], zdev(to),
+        )
 
     def z_g(to, frm):
         return remote(zg_send.at[to], zg_recv.at[frm], zg_s.at[to], zg_r.at[frm], zdev(to))
@@ -159,41 +158,62 @@
         keep_a(oy, zz)
         core_a(oy, zz).wait_recv()
         ya_send[zz] = (ca_own[oy, zz] + ca_recv[oy, zz]).astype(BF16)
-        y_a(zz).start()
+        y_a(0, zz).start()
+    for zz in order:
+        y_a(1, zz).start()
     for zz in order:
         send_a(y, zz)
         keep_a(y, zz)
     for zz in order:
         make_g(oy, zz)
+
+    def finish_a(h, i):
+        zz = order[i]
+        y_a(h, zz).wait_recv()
+        at = rows(h)
+        total = ca_own[y, zz, at] + ca_recv[y, zz, at] + ya_recv[zz, at].astype(F32)
+        if i < zs - 1:
+            za_send[zz, at] = total.astype(BF16)
+            z_a(h, zz, z).start()
+        else:
+            ca_own[y, zz, at] = total
+
     for i, zz in enumerate(order):
         core_a(y, zz).wait_recv()
-        y_a(zz).wait_recv()
-        total = ca_own[y, zz] + ca_recv[y, zz] + ya_recv[zz].astype(F32)
-        if i < zs - 1:
-            za_send[zz] = total.astype(BF16)
-            z_a(zz, z).start()
-        else:
-            ca_own[y, zz] = total
+        finish_a(0, i)
         core_g(oy, zz).wait_recv()
         yg_send[zz] = (cg_own[oy, zz] + cg_recv[oy, zz]).astype(BF16)
+    for i, zz in enumerate(order):
+        finish_a(1, i)
         y_g(zz).start()
         make_g(y, zz)
 
-    total = ca_own[y, z]
-    for zz in others:
-        z_a(z, zz).wait_recv()
-        total = total + za_recv[zz].astype(F32)
-    ag[y, z] = total.astype(BF16)
-
-    def ag_z(to, frm):
-        return remote(ag.at[y, frm], ag.at[y, frm], agz_s.at[to], agz_r.at[frm], zdev(to))
-
-    def ag_y(yy, zz):
-        return remote(ag.at[yy, zz], ag.at[yy, zz], agy_s.at[zz], agy_r.at[zz], yp)
-
-    for zz in order[:-1]:
-        ag_z(zz, z).start()
-    ag_y(y, z).start()
+    def ag_z(h, to, frm):
+        block = ag.at[y, frm, rows(h)]
+        return remote(block, block, agz_s.at[h, to], agz_r.at[h, frm], zdev(to))
+
+    def ag_y(h, yy, zz):
+        block = ag.at[yy, zz, rows(h)]
+        return remote(block, block, agy_s.at[h, zz], agy_r.at[h, zz], yp)
+
+    def gather_a(h):
+        at = rows(h)
+        total = ca_own[y, z, at]
+        for zz in others:
+            z_a(h, z, zz).wait_recv()
+            total = total + za_recv[zz, at].astype(F32)
+        ag[y, z, at] = total.astype(BF16)
+        for zz in order[:-1]:
+            ag_z(h, zz, z).start()
+        ag_y(h, y, z).start()
+
+    def forward_a(h):
+        for zz in others:
+            ag_z(h, z, zz).wait_recv()
+            ag_y(h, y, zz).start()
+
+    gather_a(0)
+    gather_a(1)
 
     def finish_g(i):
         zz = order[i]
@@ -206,12 +226,12 @@
         else:
             cg_own[y, zz] = total
 
-    for i in range(zs - 1):
+    finish_g(0)
+    finish_g(1)
+    forward_a(0)
+    for i in range(2, zs):
         finish_g(i)
-    for zz in others:
-        ag_z(z, zz).wait_recv()
-        ag_y(y, zz).start()
-    finish_g(zs - 1)
+    forward_a(1)
 
     total = cg_own[y, z]
     for zz in others:
@@ -227,7 +247,8 @@
     gout_ref[:, : CORES * half_rows] = high
     gout_ref[:, CORES * half_rows :] = (gt - high.astype(F32)).astype(BF16)
     for zz in [z] + others:
-        ag_y(oy, zz).wait_recv()
+        ag_y(0, oy, zz).wait_recv()
+        ag_y(1, oy, zz).wait_recv()
         aout_ref[oy, zz] = ag[oy, zz]
 
     def sent_tok(i, carry):
@@ -240,13 +261,17 @@
         core_g(oy, zz).wait_send()
         core_a(y, zz).wait_send()
         core_g(y, zz).wait_send()
-        y_a(zz).wait_send()
+        y_a(0, zz).wait_send()
+        y_a(1, zz).wait_send()
         y_g(zz).wait_send()
-        ag_y(y, zz).wait_send()
+        ag_y(0, y, zz).wait_send()
+        ag_y(1, y, zz).wait_send()
     for zz in order[:-1]:
-        z_a(zz, z).wait_send()
+        z_a(0, zz, z).wait_send()
+        z_a(1, zz, z).wait_send()
         z_g(zz, z).wait_send()
-        ag_z(zz, z).wait_send()
+        ag_z(0, zz, z).wait_send()
+        ag_z(1, zz, z).wait_send()
     swap.wait_send()
 
 
@@ -261,9 +286,7 @@
     gcols = width_out // ROWB
     a_grid, g_grid = (YS, zs, tokens, acols), (YS, zs, half, gcols)
     dma = pltpu.SemaphoreType.DMA
-    scratch = [pltpu.VMEM(acts.shape, BF16), pltpu.VMEM(grads.shape, BF16)]
-    scratch += [
-        pltpu.VMEM((2 * tok, width_in), BF16),
+    scratch = [
         pltpu.VMEM((tiles, 2 * tok, depth), BF16),
         pltpu.VMEM((depth, width_in), BF16),
         pltpu.VMEM((depth, width_out), BF16),
@@ -272,22 +295,23 @@
     for _ in range(2):
         scratch += [pltpu.VMEM(a_grid[1:], BF16)] * 2 + [pltpu.VMEM(g_grid[1:], BF16)] * 2
     scratch += [pltpu.VMEM(a_grid, BF16), pltpu.VMEM((CORES, half, gcols), F32)]
-    scratch += [dma((4,)), dma((tiles,)), dma((tiles,))]
-    scratch += [dma((YS, zs))] * 4 + [dma((zs,))] * 12 + [dma, dma]
+    scratch += [dma((2,)), dma((tiles,)), dma((tiles,))]
+    scratch += [dma((YS, zs))] * 4 + ([dma((2, zs))] * 2 + [dma((zs,))] * 2) * 2 + [dma((2, zs))] * 4 + [dma, dma]
     return pl.pallas_call(
         functools.partial(rotate_kernel, zs),
         out_shape=(
             jax.ShapeDtypeStruct(a_grid, BF16),
             jax.ShapeDtypeStruct((gcols, 2 * tokens), BF16),
         ),
-        in_specs=[pl.BlockSpec(memory_space=pl.ANY)] * 4,
+        in_specs=[pl.BlockSpec(memory_space=pltpu.VMEM)]
+        + [pl.BlockSpec(memory_space=pl.ANY)] * 2,
         out_specs=(pl.BlockSpec(memory_space=pltpu.VMEM),) * 2,
         scratch_shapes=scratch,
         compiler_params=pltpu.CompilerParams(
             collective_id=0, has_side_effects=True, vmem_limit_bytes=VMEM_LIMIT
         ),
         name="rotate",
-    )(acts, grads, basis_in, basis_out)
+    )(jnp.concatenate([acts, grads], axis=0), basis_in, basis_out)
 
 
 def correct_kernel(scale, a_ref, g_ref, out_ref):
@@ -313,7 +337,7 @@
             pl.BlockSpec((rows, 2 * tokens), lambda i: (0, 0)),
         ],
         out_specs=pl.BlockSpec((1, rows, step * acols), lambda i: (0, 0, i)),
-        compiler_params=pltpu.CompilerParams(vmem_limit_bytes=VMEM_LIMIT),
+        compiler_params=pltpu.CompilerParams(vmem_limit_bytes=16 * 1024 * 1024),
         name="correct",
     )(a, g)
 

time: 42.9 us -> 40.5 us (0.944)
  Pallas kernels: 42.4 us -> 39.1 us
  other arithmetic: 0 us -> 0.88 us
    pallas_call x1, Pallas kernels: 37.9 us -> 36.2 us  [rotate(): pl.pallas_call(functools.partial(rotate_kernel, zs), out_shape=(jax.Shape...]
    pallas_call x1, Pallas kernels: 4.49 us -> 2.92 us  [correct(): pl.pallas_call(functools.partial(correct_kernel, 1.0 / tokens), grid=(blo...]
    concatenate x0 -> x1, other arithmetic: none -> 0.88 us  [rotate(): jnp.concatenate([acts, grads], axis=0)]
where the time goes in v3:
time: 40.5 us; the launch traced here: 40 us
  Pallas kernels  39.1 us (97%)
  other arithmetic  0.88 us (2%)
    pallas_call x1, Pallas kernels, rotate(): pl.pallas_call(functools.partial(rotate_kernel, zs), out_shape=(jax.Shape...  36.2 us
    pallas_call x1, Pallas kernels, correct(): pl.pallas_call(functools.partial(correct_kernel, 1.0 / tokens), grid=(blo...  2.92 us
    concatenate x1, other arithmetic, rotate(): jnp.concatenate([acts, grads], axis=0)  0.88 us

profile of v3, /device:TPU:0, one launch (start us, length us, event | category | flops | bytes accessed | tf_op | source)
XLA Modules:
  0.0 40.0 jit_solution(17806157329821047218)
XLA Ops:
  0.0 0.9 %pad_maximum_fusion.x = bf16[16,4096]{1,0:T(8,128)(2,1)S(1)} fusion(bf16[8,4096]{1,0:T(8,128)(2,1)} %param.5, bf16[8,4096]{1,0:T(8,128)(2,1)} %param.4), kind=kLoop, calls=%fused_computation | loop fusion | flops 262144 | bytes 262144 | tf_op jit(solution)/shard_map/concatenate | solution.py:314
  0.9 36.2 %rotate.1 = (bf16[2,4,128,256]{3,2,1,0:T(8,128)(2,1)S(1)}, bf16[512,256]{1,0:T(8,128)(2,1)S(1)}) custom-call(bf16[16,4096]{1,0:T(8,128)(2,1)S(1)} %pad_maximum_fusion.x, bf16[256,4096]{1,0:T(8,128)(2,1)} %bin_hbm.1, bf16[256,4096]{1,0:T(8,128)(2,1)} %bout_hbm.1), custom_call_target="tpu_custom_call" | custom-call | tf_op jit(solution)/shard_map/rotate/pallas_call | solution.py:300
  37.1 2.9 %correct.1 = f32[1,512,2048]{2,1,0:T(8,128)} custom-call(bf16[8,128,256]{2,1,0:T(8,128)(2,1)S(1)} %bitcast.1, bf16[512,256]{1,0:T(8,128)(2,1)S(1)} %get-tuple-element.8.g_ref), custom_call_target="tpu_custom_call" | custom-call | tf_op jit(solution)/shard_map/correct/pallas_call | solution.py:331

commit v4 on v3

--- a/solution.py
+++ b/solution.py
@@ -166,6 +166,8 @@
         keep_a(y, zz)
     for zz in order:
         make_g(oy, zz)
+    for zz in order:
+        make_g(y, zz)
 
     def finish_a(h, i):
         zz = order[i]
@@ -186,7 +188,6 @@
     for i, zz in enumerate(order):
         finish_a(1, i)
         y_g(zz).start()
-        make_g(y, zz)
 
     def ag_z(h, to, frm):
         block = ag.at[y, frm, rows(h)]
@@ -226,9 +227,9 @@
         else:
             cg_own[y, zz] = total
 
+    forward_a(0)
     finish_g(0)
     finish_g(1)
-    forward_a(0)
     for i in range(2, zs):
         finish_g(i)
     forward_a(1)
@@ -327,7 +328,7 @@
 def correct(a, g):
     blocks, tokens, acols = a.shape
     rows = g.shape[0]
-    step = 2
+    step = 4
     return pl.pallas_call(
         functools.partial(correct_kernel, 1.0 / tokens),
         grid=(blocks // step,),

time: 40.5 us -> 40.1 us (level)
    pallas_call x1, Pallas kernels: 2.92 us -> 2.48 us  [correct(): pl.pallas_call(functools.partial(correct_kernel, 1.0 / tokens), grid=(blo...]
where the time goes in v4:
time: 40.1 us; the launch traced here: 39.6 us
  Pallas kernels  38.7 us (97%)
  other arithmetic  0.88 us (2%)
    pallas_call x1, Pallas kernels, rotate(): pl.pallas_call(functools.partial(rotate_kernel, zs), out_shape=(jax.Shape...  36.3 us
    pallas_call x1, Pallas kernels, correct(): pl.pallas_call(functools.partial(correct_kernel, 1.0 / tokens), grid=(blo...  2.48 us
    concatenate x1, other arithmetic, rotate(): jnp.concatenate([acts, grads], axis=0)  0.88 us

profile of v4, /device:TPU:0, one launch (start us, length us, event | category | flops | bytes accessed | tf_op | source)
XLA Modules:
  0.0 39.6 jit_solution(383542201044593583)
XLA Ops:
  0.0 0.9 %pad_maximum_fusion.x = bf16[16,4096]{1,0:T(8,128)(2,1)S(1)} fusion(bf16[8,4096]{1,0:T(8,128)(2,1)} %param.5, bf16[8,4096]{1,0:T(8,128)(2,1)} %param.4), kind=kLoop, calls=%fused_computation | loop fusion | flops 262144 | bytes 262144 | tf_op jit(solution)/shard_map/concatenate | solution.py:315
  0.9 36.3 %rotate.1 = (bf16[2,4,128,256]{3,2,1,0:T(8,128)(2,1)S(1)}, bf16[512,256]{1,0:T(8,128)(2,1)S(1)}) custom-call(bf16[16,4096]{1,0:T(8,128)(2,1)S(1)} %pad_maximum_fusion.x, bf16[256,4096]{1,0:T(8,128)(2,1)} %bin_hbm.1, bf16[256,4096]{1,0:T(8,128)(2,1)} %bout_hbm.1), custom_call_target="tpu_custom_call" | custom-call | tf_op jit(solution)/shard_map/rotate/pallas_call | solution.py:301
  37.1 2.5 %correct.1 = f32[1,512,2048]{2,1,0:T(8,128)} custom-call(bf16[8,128,256]{2,1,0:T(8,128)(2,1)S(1)} %bitcast.1, bf16[512,256]{1,0:T(8,128)(2,1)S(1)} %get-tuple-element.8.g_ref), custom_call_target="tpu_custom_call" | custom-call | tf_op jit(solution)/shard_map/correct/pallas_call | solution.py:332
